TPU v7x, 128 devices: a whole 4x4x4 slice. The times are simulated.
128 devices in a mesh: group: 16 (over x, z), tensor: 8 (over y, core).
Axes of the slice: x: 4, y: 4, z: 4, core: 2. Of those that a mesh axis runs over, the one named last changes fastest.
Arguments:
- queries: bfloat16 [16384, 4096], P(('group', 'tensor')), may hold values from -6 to 6
- rotated_key_rows: bfloat16 [16384, 256], P(('group', 'tensor')), may hold values from -6 to 6
- value_row_matrix: bfloat16 [16384, 256], P(('group', 'tensor')), may hold values from -12 to 12
- out_weight: bfloat16 [4096, 4096], P('tensor'), may hold values from -0.09375 to 0.09375
- residual: bfloat16 [16384, 4096], P(('group', 'tensor')), may hold values from -3 to 3
- norm_gain: float32 [4096], replicated, may hold values from 0.25 to 1.75
- expert_ids: int32 [16384, 3], P(('group', 'tensor')), may hold values from 0 to 63, all different within a row; in each aligned block of 128 rows (0 to 127, 128 to 255, ...) at most 8 rows name the same one
- gate_weights: float32 [16384, 3], P(('group', 'tensor')), may hold values from 0.05 to 0.6
- w_gate: bfloat16 [128, 4096, 768], P(('group', 'tensor')), may hold values from -0.09375 to 0.09375
- w_up: bfloat16 [128, 4096, 768], P(('group', 'tensor')), may hold values from -0.09375 to 0.09375
- w_down: bfloat16 [128, 768, 4096], P(('group', 'tensor')), may hold values from -0.15625 to 0.15625
Outputs:
- mixed: bfloat16 [16384, 4096], P(('group', 'tensor'))
Inputs may be any that keep to these rules, and one draw needn't show every extreme that they name: `expert_ids`: the 3 experts of a row differ. Among the 128 rows of one device (aligned blocks), at most 8 name one expert, and in every draw some expert is named by exactly 8 of them.
All inputs are finite; a program needn't handle non-finite values.
Results may differ from a plain program's by a relative error of at most 0.0065.
Values may be sent and summed in bfloat16 or wider, within the bound.
No kernel may reach another device: no remote copies, remote signals or barrier semaphores. Data moves between devices by JAX's collectives and lax.ppermute only.
A program may use at most 128 MiB of HBM per device.

v0:
```python
import functools

import jax
import jax.numpy as jnp
from jax import lax
from jax.experimental import pallas as pl
from jax.experimental.pallas import tpu as pltpu
from jax.sharding import Mesh
from jax.sharding import PartitionSpec as P

HEAD = 128
TOP = 3
CAP = 8
AXES = ("group", "y", "core")
LOG2E = 1.4426950408889634
ORDER = (2, 1, 3, 0)


def attend(place, core, q_ref, k_ref, v_ref, context_ref, first, unroll):
    rows = q_ref.shape[1]
    heads = q_ref.shape[2] // HEAD
    scale = HEAD ** (-0.5) * LOG2E
    for block in range(4):

        @pl.when(place == block)
        def _():
            columns = 256 * (block + 1)
            keys = k_ref[0:columns, :]
            values = v_ref[0:columns, :]
            row = lax.broadcasted_iota(jnp.int32, (2 * rows, 256), 0) % rows
            column = lax.broadcasted_iota(jnp.int32, (2 * rows, 256), 1)
            allowed = column <= row + core * rows
            def pair(index, carry):
                start = pl.multiple_of(index * 2 * HEAD, 2 * HEAD)
                both = q_ref[first, :, pl.ds(start, 2 * HEAD)]
                q = jnp.concatenate([both[:, :HEAD], both[:, HEAD:]], axis=0)
                scores = lax.dot_general(
                    q, keys, (((1,), (1,)), ((), ())), preferred_element_type=jnp.float32
                )
                last = jnp.where(allowed, scores[:, columns - 256 :], -1e30)
                if block:
                    scores = jnp.concatenate([scores[:, : columns - 256], last], axis=1)
                else:
                    scores = last
                largest = jnp.max(scores, axis=1, keepdims=True)
                weights = jnp.exp2((scores - largest) * scale).astype(jnp.bfloat16)
                context = jnp.dot(weights, values, preferred_element_type=jnp.float32)
                context = (context[:, :HEAD] / context[:, HEAD:]).astype(jnp.bfloat16)
                context_ref[pl.ds(first * rows, rows), pl.ds(start, 2 * HEAD)] = jnp.concatenate(
                    [context[:rows], context[rows:]], axis=1
                )
                return carry

            lax.fori_loop(0, heads // 2, pair, 0, unroll=unroll)


def attend_project_kernel(
    unroll, where_ref, q_ref, k_ref, v_ref, own_ref, other_ref, o_ref, context_ref
):
    @pl.when(pl.program_id(0) == 0)
    def _():
        @pl.loop(0, q_ref.shape[0])
        def _(first):
            attend(where_ref[first], where_ref[4], q_ref, k_ref, v_ref, context_ref, first, unroll)

    half = own_ref.shape[0]
    result = jnp.dot(
        context_ref[:, :half], own_ref[...], preferred_element_type=jnp.float32
    ) + jnp.dot(context_ref[:, half:], other_ref[...], preferred_element_type=jnp.float32)
    o_ref[...] = result.astype(o_ref.dtype)


def attend_project(where, queries, keys, values, weight_own, weight_other, dtype, unroll, tile=1024):
    ring, rows, depth = queries.shape
    half, width = weight_own.shape
    return pl.pallas_call(
        functools.partial(attend_project_kernel, unroll),
        out_shape=jax.ShapeDtypeStruct((ring * rows, width), dtype),
        grid_spec=pltpu.PrefetchScalarGridSpec(
            num_scalar_prefetch=1,
            grid=(width // tile,),
            in_specs=[
                pl.BlockSpec(queries.shape, lambda j, w: (0, 0, 0)),
                pl.BlockSpec(keys.shape, lambda j, w: (0, 0)),
                pl.BlockSpec(values.shape, lambda j, w: (0, 0)),
                pl.BlockSpec((half, tile), lambda j, w: (0, j)),
                pl.BlockSpec((half, tile), lambda j, w: (0, j)),
            ],
            out_specs=pl.BlockSpec((ring * rows, tile), lambda j, w: (0, j)),
            scratch_shapes=[pltpu.VMEM((ring * rows, depth), jnp.bfloat16)],
        ),
        compiler_params=pltpu.CompilerParams(vmem_limit_bytes=24 * 1024 * 1024),
        cost_estimate=pl.CostEstimate(
            flops=ring * rows * (2 * depth * width + 8 * 2560 * HEAD),
            bytes_accessed=2 * depth * width,
            transcendentals=ring * 2 * rows * 2560,
        ),
    )(where, queries, keys, values, weight_own, weight_other)


def fdot(a, b):
    return jnp.dot(a, b, preferred_element_type=jnp.float32)


def gated_kernel(tile, x_ref, gate_ref, up_ref, o_ref):
    @pl.loop(0, o_ref.shape[1] // tile)
    def _(step):
        at = pl.ds(pl.multiple_of(step * tile, tile), tile)
        gate = jnp.dot(x_ref[...], gate_ref[0, :, at], preferred_element_type=jnp.float32)
        upward = jnp.dot(x_ref[...], up_ref[0, :, at], preferred_element_type=jnp.float32)
        o_ref[:, at] = (gate / (1.0 + jnp.exp(-gate)) * upward).astype(jnp.bfloat16)


def gated(x, w_gate, w_up, tile=256):
    rows, depth = x.shape
    hidden = w_gate.shape[2]
    return pl.pallas_call(
        functools.partial(gated_kernel, tile),
        out_shape=jax.ShapeDtypeStruct((rows, hidden), jnp.bfloat16),
        in_specs=[pl.BlockSpec(memory_space=pltpu.VMEM)] * 3,
        out_specs=pl.BlockSpec(memory_space=pltpu.VMEM),
        compiler_params=pltpu.CompilerParams(vmem_limit_bytes=24 * 1024 * 1024),
        cost_estimate=pl.CostEstimate(
            flops=4 * rows * depth * hidden,
            bytes_accessed=4 * depth * hidden + 2 * rows * depth,
            transcendentals=rows * hidden,
        ),
    )(x, w_gate, w_up)


def down_kernel(tile, side, place, a_ref, w_ref, *refs):
    o_ref = refs[-1]
    half = w_ref.shape[2] // 2

    @pl.loop(0, half // tile, unroll=True)
    def _(step):
        start = pl.multiple_of(step * tile, tile)
        part = jnp.dot(
            a_ref[...],
            w_ref[0, :, pl.ds(start + side * half, tile)],
            preferred_element_type=jnp.float32,
        ).astype(jnp.bfloat16)
        if len(refs) > 1:
            added = refs[0][:, pl.ds(start, tile)].astype(jnp.float32)
            part = (part.astype(jnp.float32) + added).astype(jnp.bfloat16)
        o_ref[:, pl.ds(start + place, tile)] = part


def down(activation, w_down, side, added=None, into=None, tile=512):
    rows, hidden = activation.shape
    width = w_down.shape[2]
    whole = added is not None
    args = [a for a in (activation, w_down, added, into) if a is not None]
    return pl.pallas_call(
        functools.partial(down_kernel, tile, side, side * width // 2 if whole else 0),
        out_shape=jax.ShapeDtypeStruct((rows, width if whole else width // 2), jnp.bfloat16),
        in_specs=[pl.BlockSpec(memory_space=pltpu.VMEM)] * len(args),
        out_specs=pl.BlockSpec(memory_space=pltpu.VMEM),
        input_output_aliases={3: 0} if into is not None else {},
        compiler_params=pltpu.CompilerParams(vmem_limit_bytes=16 * 1024 * 1024),
        cost_estimate=pl.CostEstimate(
            flops=rows * hidden * width,
            bytes_accessed=hidden * width + rows * width,
            transcendentals=0,
        ),
    )(*args)


def local(
    queries,
    rotated_key_rows,
    value_row_matrix,
    out_weight,
    residual,
    norm_gain,
    expert_ids,
    gate_weights,
    w_gate,
    w_up,
    w_down,
):
    bf16, f32 = jnp.bfloat16, jnp.float32
    rows = queries.shape[0]
    width = residual.shape[1]
    ring = lax.axis_size("y")
    experts = lax.axis_size("group") * ring
    y, core = lax.axis_index("y"), lax.axis_index("core")
    other = 1 - core
    chip_width = queries.shape[1] // ring
    half_width = chip_width // 2
    half = width // 2

    def along(value, step):
        return lax.ppermute(value, "y", [(i, (i + step) % ring) for i in range(ring)])

    def swap(value):
        return lax.ppermute(value, "core", [(0, 1), (1, 0)])

    def columns(value, start, size):
        return lax.dynamic_slice_in_dim(value, start, size, axis=1)

    weight_other = swap(out_weight)

    def head_rows(step):
        to = (y + step) % ring
        start = to * rotated_key_rows.shape[1] // HEAD // ring * HEAD
        return jnp.concatenate(
            [columns(rotated_key_rows, start, HEAD), columns(value_row_matrix, start, HEAD)], axis=1
        )

    def head_queries(step):
        start = (y + step) % ring * chip_width
        return jnp.concatenate(
            [
                columns(queries, start + core * half_width, half_width),
                columns(queries, start + other * half_width, half_width),
            ],
            axis=1,
        )

    to_send = {step: head_rows(step) for step in range(ring)}
    arrived = {(-step) % ring: along(to_send[step], step) for step in (2, 1, 3)}
    arrived[0] = to_send[0]
    asked = {2: along(head_queries(2), 2)}
    key_values = jnp.stack([arrived[step] for step in range(ring)])
    key_values_other = swap(key_values)
    near = [head_queries(1), head_queries(3)]
    near, key_values_other = lax.optimization_barrier((near, key_values_other))
    asked[3] = along(near[0], 1)
    asked[1] = along(near[1], 3)
    asked[0] = head_queries(0)
    blocks = [asked[step] for step in ORDER]
    gathered = jnp.where(
        core == 0,
        jnp.stack([key_values, key_values_other], axis=1),
        jnp.stack([key_values_other, key_values], axis=1),
    )
    gathered = jnp.stack(
        [
            lax.dynamic_index_in_dim(gathered, (place - y) % ring, axis=0, keepdims=False)
            for place in range(ring)
        ]
    )
    gathered = gathered.reshape(ring * 2 * rows, 2 * HEAD)
    keys = gathered[:, :HEAD]
    values = jnp.concatenate([gathered[:, HEAD:], jnp.ones_like(keys)], axis=1)

    def attended(first, last, block, dtype, unroll):
        places = [(y + step) % ring for step in ORDER[first:last]]
        places = places + [places[0]] * (ring - len(places)) + [core]
        places = jnp.stack(places).astype(jnp.int32)
        return attend_project(places, block, keys, values, out_weight, weight_other, dtype, unroll)

    opposite = attended(0, 1, jnp.stack(blocks[:1]), bf16, 4)
    from_left = along(opposite[:, :half], 1)
    from_right = along(opposite[:, half:], -1)
    near, opposite = lax.optimization_barrier((blocks[1:3], opposite))
    near = jnp.stack(near)
    partial = attended(1, 3, near, bf16, 2)
    right, left = partial[:rows], partial[rows:]
    right_plain = along(right[:, half:], 1)
    left_plain = along(left[:, :half], -1)
    from_left, from_right, partial = lax.optimization_barrier((from_left, from_right, partial))
    right_sum = along((partial[:rows, :half].astype(f32) + from_left.astype(f32)).astype(bf16), 1)
    left_sum = along((partial[rows:, half:].astype(f32) + from_right.astype(f32)).astype(bf16), -1)
    last, _ = lax.optimization_barrier((jnp.stack(blocks[3:]), partial))
    own = attended(3, 4, last, f32, 1)
    hidden = residual.astype(f32) + own
    hidden = hidden + jnp.concatenate(
        [
            right_sum.astype(f32) + left_plain.astype(f32),
            right_plain.astype(f32) + left_sum.astype(f32),
        ],
        axis=1,
    )

    mean_square = jnp.mean(hidden * hidden, axis=-1, keepdims=True)
    moe_input = (hidden * lax.rsqrt(mean_square + 1e-06) * norm_gain).astype(bf16)

    flat_ids = expert_ids.reshape(-1)
    one_hot = (flat_ids[:, None] == jnp.arange(experts, dtype=jnp.int32)[None, :]).astype(jnp.int32)
    earlier = jnp.cumsum(one_hot, axis=0) - one_hot
    rank_within = jnp.sum(earlier * one_hot, axis=1)
    slot_index = (flat_ids * CAP + rank_within).reshape(rows, TOP)
    slot_rows = jnp.arange(experts * CAP, dtype=jnp.int32)
    hit = [slot_rows[:, None] == slot_index[:, k][None, :] for k in range(TOP)]
    selector = (hit[0] | hit[1] | hit[2]).astype(bf16)
    spread = sum(
        jnp.where(slot_rows[None, :] == slot_index[:, k][:, None], gate_weights[:, k][:, None], 0.0)
        for k in range(TOP)
    )
    spread_high = spread.astype(bf16)
    spread_low = (spread - spread_high.astype(f32)).astype(bf16)
    spread = jnp.concatenate([spread_high, spread_low], axis=0)

    slots = fdot(selector, moe_input).astype(bf16).reshape(experts, CAP, width)
    mine = lax.all_to_all(slots, ("group", "y"), split_axis=0, concat_axis=0, tiled=True)
    mine = mine.reshape(experts * CAP, width)
    theirs = swap(mine)

    active_mine = gated(mine, w_gate, w_up)
    theirs, active_mine = lax.optimization_barrier((theirs, active_mine))
    active_theirs = gated(theirs, w_gate, w_up)
    back = [swap(down(active_theirs, w_down, side)) for side in (0, 1)]
    expert_out = down(active_mine, w_down, 0, back[0])
    expert_out = down(active_mine, w_down, 1, back[1], expert_out)
    expert_out, spread, hidden = lax.optimization_barrier((expert_out, spread, hidden))
    returned = lax.all_to_all(
        expert_out.reshape(experts, CAP, width),
        ("group", "y"),
        split_axis=0,
        concat_axis=0,
        tiled=True,
    ).reshape(experts * CAP, width)
    routed = fdot(spread, returned)
    return (hidden + routed[:rows] + routed[rows:]).astype(bf16)


def solution(mesh):
    devices = mesh.devices
    mesh = Mesh(devices.reshape(devices.shape[0], devices.shape[1] // 2, 2), AXES)
    wide = P(AXES, None)
    deep = P(AXES, None, None)
    return jax.shard_map(
        local,
        mesh=mesh,
        in_specs=(
            wide,
            wide,
            wide,
            P(("y", "core"), None),
            wide,
            P(),
            wide,
            wide,
            deep,
            deep,
            deep,
        ),
        out_specs=wide,
        check_vma=False,
    )
```

profile of v0, /device:TPU:1, one launch (start us, length us, event | category | flops | bytes accessed | tf_op | source)
XLA Modules:
  0.0 213.0 jit_solution(17717643222058643040)
XLA Ops:
  0.0 1.4 collective-permute-start.5
  2.4 2.9 %collective-permute-start.1 = (bf16[128,256]{1,0:T(8,128)(2,1)S(1)}, bf16[128,256]{1,0:T(8,128)(2,1)S(1)}, u32[]{:S(2)}, u32[]{:S(2)}) collective-permute-start(bf16[128,256]{1,0:T(8,128)(2,1)S(1)} %pad_maximum_fusion.7), channel_id=1, source_target_pairs={{0,6},{2,0},{4,2},{6,4},{1,7},{3,1},{5,3},{7,5},{8,14},{10,8},{12,... | collective-permute-start | bytes 196616 | tf_op jit(solution)/shard_map/ppermute | solution.py:194
  6.6 2.1 collective-permute-start
  10.0 2.2 %collective-permute-done.3 = bf16[128,256]{1,0:T(8,128)(2,1)S(1)} collective-permute-done((bf16[128,256]{1,0:T(8,128)(2,1)S(1)}, bf16[128,256]{1,0:T(8,128)(2,1)S(1)}, u32[]{:S(2)}, u32[]{:S(2)}) %collective-permute-start.3) | collective-permute-done | bytes 65568 | tf_op jit(solution)/shard_map/ppermute | solution.py:194
  12.3 1.6 collective-permute-start.4
  17.4 6.1 %shard_map.109 = bf16[128,4096]{1,0:T(8,128)(2,1)S(1)} custom-call(s32[5]{0:T(128)S(1)} %stack.90.where_ref, bf16[1,128,1024]{2,1,0:T(8,128)(2,1)S(1)} %bitcast.64, bf16[1024,128]{1,0:T(8,128)(2,1)S(1)} %get-tuple-element.50.k_ref, bf16[1024,256]{1,0:T(8,128)(2,1)S(1)} %concatenate.41.v_ref, bf16[512,4096]{1,0:T(8,128)(2,1)S(1)} %copy-done, ...), custom_call_target="tpu_custom_call" | custom-call | flops 1409286144 | bytes 8388608 | tf_op jit(solution)/shard_map/pallas_call | solution.py:76
  23.6 3.6 %collective-permute-done.9 = bf16[128,1024]{1,0:T(8,128)(2,1)S(1)} collective-permute-done((bf16[128,1024]{1,0:T(8,128)(2,1)S(1)}, bf16[128,1024]{1,0:T(8,128)(2,1)S(1)}, u32[]{:S(2)}, u32[]{:S(2)}) %collective-permute-start.9) | collective-permute-done | bytes 262176 | tf_op jit(solution)/shard_map/ppermute | solution.py:194
  27.3 2.5 %collective-permute-start.7 = (bf16[128,2048]{1,0:T(8,128)(2,1)S(1)}, bf16[128,2048]{1,0:T(8,128)(2,1)S(1)}, u32[]{:S(2)}, u32[]{:S(2)}) collective-permute-start(bf16[128,2048]{1,0:T(8,128)(2,1)S(1)} %get-tuple-element.47), channel_id=1, source_target_pairs={{0,6},{2,0},{4,2},{6,4},{1,7},{3,1},{5,3},{7,5},{8,14},{10,8},{12,... | collective-permute-start | bytes 1572872 | tf_op jit(solution)/shard_map/ppermute | solution.py:194
  29.9 9.3 %shard_map.110 = bf16[256,4096]{1,0:T(8,128)(2,1)S(1)} custom-call(s32[5]{0:T(128)S(1)} %stack.104.where_ref, bf16[2,128,1024]{2,1,0:T(8,128)(2,1)S(1)} %pad_maximum_fusion.1.q_ref, bf16[1024,128]{1,0:T(8,128)(2,1)S(1)} %get-tuple-element.50.k_ref, bf16[1024,256]{1,0:T(8,128)(2,1)S(1)} %concatenate.41.v_ref, bf16[512,4096]{1,0:T(8,128)(2,1)S(1)} %copy-done, ...), custom_call_target="tpu_custom_call" | custom-call | flops 2818572288 | bytes 8388608 | tf_op jit(solution)/shard_map/pallas_call | solution.py:76
  42.3 2.6 %collective-permute-start.13 = (bf16[128,2048]{1,0:T(8,128)(2,1)S(1)}, bf16[128,2048]{1,0:T(8,128)(2,1)S(1)}, u32[]{:S(2)}, u32[]{:S(2)}) collective-permute-start(bf16[128,2048]{1,0:T(8,128)(2,1)S(1)} %get-tuple-element.36), channel_id=1, source_target_pairs={{0,6},{2,0},{4,2},{6,4},{1,7},{3,1},{5,3},{7,5},{8,14},{10,8},{12,... | collective-permute-start | bytes 1572872 | tf_op jit(solution)/shard_map/ppermute | solution.py:194
  44.9 2.2 %copy-done.1 = bf16[512,4096]{1,0:T(8,128)(2,1)S(1)} copy-done((bf16[512,4096]{1,0:T(8,128)(2,1)S(1)}, bf16[512,4096]{1,0:T(8,128)(2,1)}, u32[]{:S(2)}) %copy-start.1) | copy-done | bytes 4194328
  47.1 6.5 %shard_map.111 = f32[128,4096]{1,0:T(8,128)S(1)} custom-call(s32[5]{0:T(128)S(1)} %stack.87.where_ref, bf16[1,128,1024]{2,1,0:T(8,128)(2,1)S(1)} %maximum_bitcast_fusion.q_ref, bf16[1024,128]{1,0:T(8,128)(2,1)S(1)} %get-tuple-element.50.k_ref, bf16[1024,256]{1,0:T(8,128)(2,1)S(1)} %concatenate.41.v_ref, bf16[512,4096]{1,0:T(8,128)(2,1)S(1)} %copy-done.1, ...), custom_call_target="tpu_custom_call" | custom-call | flops 1409286144 | bytes 8388608 | tf_op jit(solution)/shard_map/pallas_call | solution.py:76
  54.9 9.5 %collective-permute-done.12 = bf16[128,2048]{1,0:T(8,128)(2,1)S(1)} collective-permute-done((bf16[128,2048]{1,0:T(8,128)(2,1)S(1)}, bf16[128,2048]{1,0:T(8,128)(2,1)S(1)}, u32[]{:S(2)}, u32[]{:S(2)}) %collective-permute-start.12) | collective-permute-done | bytes 524320 | tf_op jit(solution)/shard_map/ppermute | solution.py:194
  66.5 58.5 %all_to_all.10 = bf16[64,8,4096]{2,1,0:T(8,128)(2,1)S(1)} all-to-all(bf16[64,8,4096]{2,1,0:T(8,128)(2,1)S(1)} %fusion), channel_id=1, replica_groups=mesh['group'=16,'y'=4,'core'=2] {'group','y'}, dimensions={0} | all-to-all | bytes 8388608 | tf_op jit(solution)/shard_map/all_to_all | solution.py:297
  125.0 4.3 %collective-permute-start.14 = (bf16[512,4096]{1,0:T(8,128)(2,1)S(1)}, bf16[512,4096]{1,0:T(8,128)(2,1)S(1)}, u32[]{:S(2)}, u32[]{:S(2)}) collective-permute-start(bf16[512,4096]{1,0:T(8,128)(2,1)S(1)} %bitcast.62), channel_id=1, source_target_pairs={{0,1},{1,0},{2,3},{3,2},{4,5},{5,4},{6,7},{7,6},{8,9},{9,8},{10,11... | collective-permute-start | bytes 12582920 | tf_op jit(solution)/shard_map/ppermute | solution.py:197
  129.3 7.2 %shard_map.112.a_ref = bf16[512,768]{1,0:T(8,128)(2,1)S(1)} custom-call(bf16[512,4096]{1,0:T(8,128)(2,1)S(1)} %bitcast.63, bf16[1,4096,768]{2,1,0:T(8,128)(2,1)S(1)} %bitcast.66, bf16[1,4096,768]{2,1,0:T(8,128)(2,1)S(1)} %bitcast.68), custom_call_target="tpu_custom_call" | custom-call | flops 6442450944 | bytes 16777216 | tf_op jit(solution)/shard_map/pallas_call | solution.py:117
  136.5 7.2 %shard_map.113.a_ref = bf16[512,768]{1,0:T(8,128)(2,1)S(1)} custom-call(bf16[512,4096]{1,0:T(8,128)(2,1)S(1)} %collective-permute-done.14.x_ref, bf16[1,4096,768]{2,1,0:T(8,128)(2,1)S(1)} %bitcast.66, bf16[1,4096,768]{2,1,0:T(8,128)(2,1)S(1)} %bitcast.68), custom_call_target="tpu_custom_call" | custom-call | flops 6442450944 | bytes 16777216 | tf_op jit(solution)/shard_map/pallas_call | solution.py:117
  143.8 1.8 shard_map.115
  145.7 1.8 shard_map.114
  148.3 1.6 collective-permute-done.16.refs_0_
  149.8 1.8 shard_map.116.refs_1_
  152.8 1.8 shard_map.117
  154.7 55.6 %all_to_all.11 = bf16[64,8,4096]{2,1,0:T(8,128)(2,1)S(1)} all-to-all(bf16[64,8,4096]{2,1,0:T(8,128)(2,1)S(1)} %bitcast.61), channel_id=1, replica_groups=mesh['group'=16,'y'=4,'core'=2] {'group','y'}, dimensions={0} | all-to-all | bytes 8388608 | tf_op jit(solution)/shard_map/all_to_all | solution.py:308
  211.6 1.4 fusion.3
  (95 shorter events, 16.8 us)
Async XLA Ops:
  0.0 17.0 %collective-permute-start.5 = (bf16[512,4096]{1,0:T(8,128)(2,1)}, bf16[512,4096]{1,0:T(8,128)(2,1)}, u32[]{:S(2)}, u32[]{:S(2)}) collective-permute-start(bf16[512,4096]{1,0:T(8,128)(2,1)} %own_ref.5), channel_id=1, source_target_pairs={{0,1},{1,0},{2,3},{3,2},{4,5},{5,4},{6,7},{7,6},{8,9},{9,8},{10,11... | collective-permute-start | bytes 12582920 | tf_op jit(solution)/shard_map/ppermute | solution.py:197
  2.4 7.6 %collective-permute-start.1 = (bf16[128,256]{1,0:T(8,128)(2,1)S(1)}, bf16[128,256]{1,0:T(8,128)(2,1)S(1)}, u32[]{:S(2)}, u32[]{:S(2)}) collective-permute-start(bf16[128,256]{1,0:T(8,128)(2,1)S(1)} %pad_maximum_fusion.7), channel_id=1, source_target_pairs={{0,6},{2,0},{4,2},{6,4},{1,7},{3,1},{5,3},{7,5},{8,14},{10,8},{12,... | collective-permute-start | bytes 196616 | tf_op jit(solution)/shard_map/ppermute | solution.py:194
  5.3 4.8 %collective-permute-start.2 = (bf16[128,256]{1,0:T(8,128)(2,1)S(1)}, bf16[128,256]{1,0:T(8,128)(2,1)S(1)}, u32[]{:S(2)}, u32[]{:S(2)}) collective-permute-start(bf16[128,256]{1,0:T(8,128)(2,1)S(1)} %pad_maximum_fusion.8), channel_id=1, source_target_pairs={{0,4},{2,6},{4,0},{6,2},{1,5},{3,7},{5,1},{7,3},{8,12},{10,14},{12... | collective-permute-start | bytes 196616 | tf_op jit(solution)/shard_map/ppermute | solution.py:194
  5.7 6.5 %collective-permute-start.3 = (bf16[128,256]{1,0:T(8,128)(2,1)S(1)}, bf16[128,256]{1,0:T(8,128)(2,1)S(1)}, u32[]{:S(2)}, u32[]{:S(2)}) collective-permute-start(bf16[128,256]{1,0:T(8,128)(2,1)S(1)} %pad_maximum_fusion.9), channel_id=1, source_target_pairs={{0,2},{2,4},{4,6},{6,0},{1,3},{3,5},{5,7},{7,1},{8,10},{10,12},{12... | collective-permute-start | bytes 196616 | tf_op jit(solution)/shard_map/ppermute | solution.py:194
  6.6 10.4 %collective-permute-start = (bf16[128,1024]{1,0:T(8,128)(2,1)S(1)}, bf16[128,1024]{1,0:T(8,128)(2,1)S(1)}, u32[]{:S(2)}, u32[]{:S(2)}) collective-permute-start(bf16[128,1024]{1,0:T(8,128)(2,1)S(1)} %pad_maximum_fusion.2), channel_id=1, source_target_pairs={{0,4},{2,6},{4,0},{6,2},{1,5},{3,7},{5,1},{7,3},{8,12},{10,14},{12... | collective-permute-start | bytes 786440 | tf_op jit(solution)/shard_map/ppermute | solution.py:194
  12.3 2.8 %collective-permute-start.4 = (bf16[4,128,256]{2,1,0:T(8,128)(2,1)S(1)}, bf16[4,128,256]{2,1,0:T(8,128)(2,1)S(1)}, u32[]{:S(2)}, u32[]{:S(2)}) collective-permute-start(bf16[4,128,256]{2,1,0:T(8,128)(2,1)S(1)} %get-tuple-element.56), channel_id=1, source_target_pairs={{0,1},{1,0},{2,3},{3,2},{4,5},{5,4},{6,7},{7,6},{8,9},{9,8},{10,11... | collective-permute-start | bytes 786440 | tf_op jit(solution)/shard_map/ppermute | solution.py:197
  15.4 8.2 %collective-permute-start.8 = (bf16[128,1024]{1,0:T(8,128)(2,1)S(1)}, bf16[128,1024]{1,0:T(8,128)(2,1)S(1)}, u32[]{:S(2)}, u32[]{:S(2)}) collective-permute-start(bf16[128,1024]{1,0:T(8,128)(2,1)S(1)} %get-tuple-element.20), channel_id=1, source_target_pairs={{0,6},{2,0},{4,2},{6,4},{1,7},{3,1},{5,3},{7,5},{8,14},{10,8},{12,... | collective-permute-start | bytes 786440 | tf_op jit(solution)/shard_map/ppermute | solution.py:194
  15.7 11.4 %collective-permute-start.9 = (bf16[128,1024]{1,0:T(8,128)(2,1)S(1)}, bf16[128,1024]{1,0:T(8,128)(2,1)S(1)}, u32[]{:S(2)}, u32[]{:S(2)}) collective-permute-start(bf16[128,1024]{1,0:T(8,128)(2,1)S(1)} %get-tuple-element.21), channel_id=1, source_target_pairs={{0,2},{2,4},{4,6},{6,0},{1,3},{3,5},{5,7},{7,1},{8,10},{10,12},{12... | collective-permute-start | bytes 786440 | tf_op jit(solution)/shard_map/ppermute | solution.py:194
  27.2 13.4 %collective-permute-start.6 = (bf16[128,2048]{1,0:T(8,128)(2,1)S(1)}, bf16[128,2048]{1,0:T(8,128)(2,1)S(1)}, u32[]{:S(2)}, u32[]{:S(2)}) collective-permute-start(bf16[128,2048]{1,0:T(8,128)(2,1)S(1)} %get-tuple-element.48), channel_id=1, source_target_pairs={{0,2},{2,4},{4,6},{6,0},{1,3},{3,5},{5,7},{7,1},{8,10},{10,12},{12... | collective-permute-start | bytes 1572872 | tf_op jit(solution)/shard_map/ppermute | solution.py:194
  27.3 13.3 %collective-permute-start.7 = (bf16[128,2048]{1,0:T(8,128)(2,1)S(1)}, bf16[128,2048]{1,0:T(8,128)(2,1)S(1)}, u32[]{:S(2)}, u32[]{:S(2)}) collective-permute-start(bf16[128,2048]{1,0:T(8,128)(2,1)S(1)} %get-tuple-element.47), channel_id=1, source_target_pairs={{0,6},{2,0},{4,2},{6,4},{1,7},{3,1},{5,3},{7,5},{8,14},{10,8},{12,... | collective-permute-start | bytes 1572872 | tf_op jit(solution)/shard_map/ppermute | solution.py:194
  39.3 14.3 %collective-permute-start.11 = (bf16[128,2048]{1,0:T(8,128)(2,1)S(1)}, bf16[128,2048]{1,0:T(8,128)(2,1)S(1)}, u32[]{:S(2)}, u32[]{:S(2)}) collective-permute-start(bf16[128,2048]{1,0:T(8,128)(2,1)S(1)} %get-tuple-element.37), channel_id=1, source_target_pairs={{0,6},{2,0},{4,2},{6,4},{1,7},{3,1},{5,3},{7,5},{8,14},{10,8},{12,... | collective-permute-start | bytes 1572872 | tf_op jit(solution)/shard_map/ppermute | solution.py:194
  41.8 11.9 %collective-permute-start.10 = (bf16[128,2048]{1,0:T(8,128)(2,1)}, bf16[128,2048]{1,0:T(8,128)(2,1)}, u32[]{:S(2)}, u32[]{:S(2)}) collective-permute-start(bf16[128,2048]{1,0:T(8,128)(2,1)} %get-tuple-element.35), channel_id=1, source_target_pairs={{0,2},{2,4},{4,6},{6,0},{1,3},{3,5},{5,7},{7,1},{8,10},{10,12},{12... | collective-permute-start | bytes 1572872 | tf_op jit(solution)/shard_map/ppermute | solution.py:194
  42.1 22.3 %collective-permute-start.12 = (bf16[128,2048]{1,0:T(8,128)(2,1)S(1)}, bf16[128,2048]{1,0:T(8,128)(2,1)S(1)}, u32[]{:S(2)}, u32[]{:S(2)}) collective-permute-start(bf16[128,2048]{1,0:T(8,128)(2,1)S(1)} %get-tuple-element.38), channel_id=1, source_target_pairs={{0,2},{2,4},{4,6},{6,0},{1,3},{3,5},{5,7},{7,1},{8,10},{10,12},{12... | collective-permute-start | bytes 1572872 | tf_op jit(solution)/shard_map/ppermute | solution.py:194
  42.3 22.1 %collective-permute-start.13 = (bf16[128,2048]{1,0:T(8,128)(2,1)S(1)}, bf16[128,2048]{1,0:T(8,128)(2,1)S(1)}, u32[]{:S(2)}, u32[]{:S(2)}) collective-permute-start(bf16[128,2048]{1,0:T(8,128)(2,1)S(1)} %get-tuple-element.36), channel_id=1, source_target_pairs={{0,6},{2,0},{4,2},{6,4},{1,7},{3,1},{5,3},{7,5},{8,14},{10,8},{12,... | collective-permute-start | bytes 1572872 | tf_op jit(solution)/shard_map/ppermute | solution.py:194
  53.6 10.9 %copy-start.3 = (bf16[128,4096]{1,0:T(8,128)(2,1)S(1)}, bf16[128,4096]{1,0:T(8,128)(2,1)}, u32[]{:S(2)}) copy-start(bf16[128,4096]{1,0:T(8,128)(2,1)} %param.15) | copy-start | bytes 3145732
  64.6 64.7 %slice-start.2 = ((s8[6291456]{0:T(1024)(128)(4,1)}), s8[4194304]{0:T(1024)(128)(4,1)S(1)}, s32[]{:S(2)}) async-start(s8[6291456]{0:T(1024)(128)(4,1)} %bitcast.65), calls=%async_computation.4 | async-start | bytes 8388608
  64.6 64.7 %slice-start.4 = ((s8[6291456]{0:T(1024)(128)(4,1)}), s8[4194304]{0:T(1024)(128)(4,1)S(1)}, s32[]{:S(2)}) async-start(s8[6291456]{0:T(1024)(128)(4,1)} %bitcast.67), calls=%async_computation.6 | async-start | bytes 8388608
  65.1 64.2 %slice-start.3 = ((s8[6291456]{0:T(1024)(128)(4,1)}), s8[2097152]{0:T(1024)(128)(4,1)S(1)}, s32[]{:S(2)}) async-start(s8[6291456]{0:T(1024)(128)(4,1)} %bitcast.65), calls=%async_computation.5 | async-start | bytes 4194304
  65.2 64.1 %slice-start.5 = ((s8[6291456]{0:T(1024)(128)(4,1)}), s8[2097152]{0:T(1024)(128)(4,1)S(1)}, s32[]{:S(2)}) async-start(s8[6291456]{0:T(1024)(128)(4,1)} %bitcast.67), calls=%async_computation.7 | async-start | bytes 4194304
  66.5 77.2 %slice-start = ((s8[6291456]{0:T(1024)(128)(4,1)}), s8[4194304]{0:T(1024)(128)(4,1)S(1)}, s32[]{:S(2)}) async-start(s8[6291456]{0:T(1024)(128)(4,1)} %bitcast.59), calls=%async_computation.2 | async-start | bytes 8388608
  125.0 18.7 %slice-start.1 = ((s8[6291456]{0:T(1024)(128)(4,1)}), s8[2097152]{0:T(1024)(128)(4,1)S(1)}, s32[]{:S(2)}) async-start(s8[6291456]{0:T(1024)(128)(4,1)} %bitcast.59), calls=%async_computation.3 | async-start | bytes 4194304
  125.0 11.5 %collective-permute-start.14 = (bf16[512,4096]{1,0:T(8,128)(2,1)S(1)}, bf16[512,4096]{1,0:T(8,128)(2,1)S(1)}, u32[]{:S(2)}, u32[]{:S(2)}) collective-permute-start(bf16[512,4096]{1,0:T(8,128)(2,1)S(1)} %bitcast.62), channel_id=1, source_target_pairs={{0,1},{1,0},{2,3},{3,2},{4,5},{5,4},{6,7},{7,6},{8,9},{9,8},{10,11... | collective-permute-start | bytes 12582920 | tf_op jit(solution)/shard_map/ppermute | solution.py:197
  145.6 4.2 %collective-permute-start.16 = (bf16[512,2048]{1,0:T(8,128)(2,1)S(1)}, bf16[512,2048]{1,0:T(8,128)(2,1)S(1)}, u32[]{:S(2)}, u32[]{:S(2)}) collective-permute-start(bf16[512,2048]{1,0:T(8,128)(2,1)S(1)} %shard_map.115), channel_id=1, source_target_pairs={{0,1},{1,0},{2,3},{3,2},{4,5},{5,4},{6,7},{7,6},{8,9},{9,8},{10,11... | collective-permute-start | bytes 6291464 | tf_op jit(solution)/shard_map/ppermute | solution.py:197
  147.5 5.3 %collective-permute-start.15 = (bf16[512,2048]{1,0:T(8,128)(2,1)S(1)}, bf16[512,2048]{1,0:T(8,128)(2,1)S(1)}, u32[]{:S(2)}, u32[]{:S(2)}) collective-permute-start(bf16[512,2048]{1,0:T(8,128)(2,1)S(1)} %shard_map.114), channel_id=1, source_target_pairs={{0,1},{1,0},{2,3},{3,2},{4,5},{5,4},{6,7},{7,6},{8,9},{9,8},{10,11... | collective-permute-start | bytes 6291464 | tf_op jit(solution)/shard_map/ppermute | solution.py:197
  (6 other events, 22.8 us)
where the time goes:
time: 215 us; the launch traced here: 213 us
  blocking collectives  114 us (53%)
  Pallas kernels  43.6 us (20%)
  starting transfers between devices  21.5 us (10%)
  waiting for transfers between devices  19.3 us (9%)
  other arithmetic  6.12 us (3%)
  local copies, waits for them, and re-layouts  5.25 us (2%)
  matrix products  2.6 us (1%)
    all_to_all x1, blocking collectives, local(): lax.all_to_all(slots, ('group', 'y'), split_axis=0, concat_axis=0, tiled=...  58.5 us
    all_to_all x1, blocking collectives, local(): lax.all_to_all(expert_out.reshape(experts, CAP, width), ('group', 'y'), s...  55.6 us
    pallas_call x3, Pallas kernels, attend_project(): pl.pallas_call(functools.partial(attend_project_kernel, unroll), out_shap...  22 us
    ppermute x12, waiting for transfers between devices, along(): lax.ppermute(value, 'y', [(i, (i + step) % ring) for i in range(ring)])  16.5 us
    pallas_call x2, Pallas kernels, gated(): pl.pallas_call(functools.partial(gated_kernel, tile), out_shape=jax.Shape...  14.4 us
    ppermute x12, starting transfers between devices, along(): lax.ppermute(value, 'y', [(i, (i + step) % ring) for i in range(ring)])  13.5 us
    ppermute x5, starting transfers between devices, swap(): return lax.ppermute(value, 'core', [(0, 1), (1, 0)])  7.98 us
    pallas_call x4, Pallas kernels, down(): pl.pallas_call(functools.partial(down_kernel, tile, side, side * width //...  7.26 us
  transfers between devices with their start and end apart: 17, of which 6 were waited for; matrix products, arithmetic and copies ran while one was open for 3% of the time, Pallas kernels for 15%

commit v1 on v0

--- a/solution.py
+++ b/solution.py
@@ -14,6 +14,7 @@
 AXES = ("group", "y", "core")
 LOG2E = 1.4426950408889634
 ORDER = (2, 1, 3, 0)
+PARTS = 4
 
 
 def attend(place, core, q_ref, k_ref, v_ref, context_ref, first, unroll):
@@ -130,14 +131,14 @@
 
 def down_kernel(tile, side, place, a_ref, w_ref, *refs):
     o_ref = refs[-1]
-    half = w_ref.shape[2] // 2
-
-    @pl.loop(0, half // tile, unroll=True)
+    some = w_ref.shape[2] // PARTS
+
+    @pl.loop(0, some // tile, unroll=True)
     def _(step):
         start = pl.multiple_of(step * tile, tile)
         part = jnp.dot(
             a_ref[...],
-            w_ref[0, :, pl.ds(start + side * half, tile)],
+            w_ref[0, :, pl.ds(start + side * some, tile)],
             preferred_element_type=jnp.float32,
         ).astype(jnp.bfloat16)
         if len(refs) > 1:
@@ -152,15 +153,15 @@
     whole = added is not None
     args = [a for a in (activation, w_down, added, into) if a is not None]
     return pl.pallas_call(
-        functools.partial(down_kernel, tile, side, side * width // 2 if whole else 0),
-        out_shape=jax.ShapeDtypeStruct((rows, width if whole else width // 2), jnp.bfloat16),
+        functools.partial(down_kernel, tile, side, side * width // PARTS if whole else 0),
+        out_shape=jax.ShapeDtypeStruct((rows, width if whole else width // PARTS), jnp.bfloat16),
         in_specs=[pl.BlockSpec(memory_space=pltpu.VMEM)] * len(args),
         out_specs=pl.BlockSpec(memory_space=pltpu.VMEM),
         input_output_aliases={3: 0} if into is not None else {},
         compiler_params=pltpu.CompilerParams(vmem_limit_bytes=16 * 1024 * 1024),
         cost_estimate=pl.CostEstimate(
-            flops=rows * hidden * width,
-            bytes_accessed=hidden * width + rows * width,
+            flops=2 * rows * hidden * width // PARTS,
+            bytes_accessed=2 * (hidden + rows) * width // PARTS,
             transcendentals=0,
         ),
     )(*args)
@@ -219,13 +220,12 @@
         )
 
     to_send = {step: head_rows(step) for step in range(ring)}
+    asked = {2: along(head_queries(2), 2)}
     arrived = {(-step) % ring: along(to_send[step], step) for step in (2, 1, 3)}
     arrived[0] = to_send[0]
-    asked = {2: along(head_queries(2), 2)}
     key_values = jnp.stack([arrived[step] for step in range(ring)])
     key_values_other = swap(key_values)
     near = [head_queries(1), head_queries(3)]
-    near, key_values_other = lax.optimization_barrier((near, key_values_other))
     asked[3] = along(near[0], 1)
     asked[1] = along(near[1], 3)
     asked[0] = head_queries(0)
@@ -294,6 +294,7 @@
     spread = jnp.concatenate([spread_high, spread_low], axis=0)
 
     slots = fdot(selector, moe_input).astype(bf16).reshape(experts, CAP, width)
+    slots, spread, hidden = lax.optimization_barrier((slots, spread, hidden))
     mine = lax.all_to_all(slots, ("group", "y"), split_axis=0, concat_axis=0, tiled=True)
     mine = mine.reshape(experts * CAP, width)
     theirs = swap(mine)
@@ -301,9 +302,10 @@
     active_mine = gated(mine, w_gate, w_up)
     theirs, active_mine = lax.optimization_barrier((theirs, active_mine))
     active_theirs = gated(theirs, w_gate, w_up)
-    back = [swap(down(active_theirs, w_down, side)) for side in (0, 1)]
-    expert_out = down(active_mine, w_down, 0, back[0])
-    expert_out = down(active_mine, w_down, 1, back[1], expert_out)
+    back = [swap(down(active_theirs, w_down, side)) for side in range(PARTS)]
+    expert_out = None
+    for side in range(PARTS):
+        expert_out = down(active_mine, w_down, side, back[side], expert_out)
     expert_out, spread, hidden = lax.optimization_barrier((expert_out, spread, hidden))
     returned = lax.all_to_all(
         expert_out.reshape(experts, CAP, width),

time: 215 us -> 213 us (level)
  waiting for transfers between devices: 19.3 us -> 10.6 us
  starting transfers between devices: 21.5 us -> 25 us
    ppermute x12, waiting for transfers between devices: 16.5 us -> 9.61 us  [along(): lax.ppermute(value, 'y', [(i, (i + step) % ring) for i in range(ring)])]
    ppermute x12, starting transfers between devices: 13.5 us -> 15.9 us  [along(): lax.ppermute(value, 'y', [(i, (i + step) % ring) for i in range(ring)])]
    ppermute x5 -> x7, starting transfers between devices: 7.98 us -> 9.03 us  [swap(): return lax.ppermute(value, 'core', [(0, 1), (1, 0)])]
    pallas_call x4 -> x8, Pallas kernels: 7.26 us -> 7.9 us  [down(): pl.pallas_call(functools.partial(down_kernel, tile, side, side * width //...]
  transfers between devices with their start and end apart: 17 -> 19, of which waited for: 6 -> 4; matrix products, arithmetic and copies ran while one was open for 3% -> 3% of each run, Pallas kernels for 15% -> 17%
where the time goes in v1:
time: 213 us; the launch traced here: 211 us
  blocking collectives  116 us (54%)
  Pallas kernels  44.3 us (21%)
  starting transfers between devices  25 us (12%)
  waiting for transfers between devices  10.6 us (5%)
  local copies, waits for them, and re-layouts  6.2 us (3%)
  other arithmetic  6.13 us (3%)
  matrix products  2.61 us (1%)
    all_to_all x1, blocking collectives, local(): lax.all_to_all(slots, ('group', 'y'), split_axis=0, concat_axis=0, tiled=...  59.3 us
    all_to_all x1, blocking collectives, local(): lax.all_to_all(expert_out.reshape(experts, CAP, width), ('group', 'y'), s...  56.8 us
    pallas_call x3, Pallas kernels, attend_project(): pl.pallas_call(functools.partial(attend_project_kernel, unroll), out_shap...  22 us
    ppermute x12, starting transfers between devices, along(): lax.ppermute(value, 'y', [(i, (i + step) % ring) for i in range(ring)])  15.9 us
    pallas_call x2, Pallas kernels, gated(): pl.pallas_call(functools.partial(gated_kernel, tile), out_shape=jax.Shape...  14.4 us
    ppermute x12, waiting for transfers between devices, along(): lax.ppermute(value, 'y', [(i, (i + step) % ring) for i in range(ring)])  9.61 us
    ppermute x7, starting transfers between devices, swap(): return lax.ppermute(value, 'core', [(0, 1), (1, 0)])  9.03 us
    pallas_call x8, Pallas kernels, down(): pl.pallas_call(functools.partial(down_kernel, tile, side, side * width //...  7.9 us
  transfers between devices with their start and end apart: 19, of which 4 were waited for; matrix products, arithmetic and copies ran while one was open for 3% of the time, Pallas kernels for 17%

profile of v1, /device:TPU:1, one launch (start us, length us, event | category | flops | bytes accessed | tf_op | source)
XLA Modules:
  0.0 211.4 jit_solution(5847625183409004299)
XLA Ops:
  0.0 1.4 collective-permute-start.5
  2.4 2.9 %collective-permute-start.1 = (bf16[128,256]{1,0:T(8,128)(2,1)S(1)}, bf16[128,256]{1,0:T(8,128)(2,1)S(1)}, u32[]{:S(2)}, u32[]{:S(2)}) collective-permute-start(bf16[128,256]{1,0:T(8,128)(2,1)S(1)} %pad_maximum_fusion.7), channel_id=1, source_target_pairs={{0,6},{2,0},{4,2},{6,4},{1,7},{3,1},{5,3},{7,5},{8,14},{10,8},{12,... | collective-permute-start | bytes 196616 | tf_op jit(solution)/shard_map/ppermute | solution.py:195
  6.6 2.1 collective-permute-start
  11.0 2.0 collective-permute-start.8
  13.1 1.8 collective-permute-start.4
  17.0 1.3 copy-done
  18.3 6.1 %shard_map.109 = bf16[128,4096]{1,0:T(8,128)(2,1)S(1)} custom-call(s32[5]{0:T(128)S(1)} %stack.90.where_ref, bf16[1,128,1024]{2,1,0:T(8,128)(2,1)S(1)} %bitcast.64, bf16[1024,128]{1,0:T(8,128)(2,1)S(1)} %get-tuple-element.50.k_ref, bf16[1024,256]{1,0:T(8,128)(2,1)S(1)} %concatenate.39.v_ref, bf16[512,4096]{1,0:T(8,128)(2,1)S(1)} %copy-done, ...), custom_call_target="tpu_custom_call" | custom-call | flops 1409286144 | bytes 8388608 | tf_op jit(solution)/shard_map/pallas_call | solution.py:77
  25.2 2.2 %collective-permute-start.7 = (bf16[128,2048]{1,0:T(8,128)(2,1)S(1)}, bf16[128,2048]{1,0:T(8,128)(2,1)S(1)}, u32[]{:S(2)}, u32[]{:S(2)}) collective-permute-start(bf16[128,2048]{1,0:T(8,128)(2,1)S(1)} %get-tuple-element.47), channel_id=1, source_target_pairs={{0,6},{2,0},{4,2},{6,4},{1,7},{3,1},{5,3},{7,5},{8,14},{10,8},{12,... | collective-permute-start | bytes 1572872 | tf_op jit(solution)/shard_map/ppermute | solution.py:195
  27.4 9.3 %shard_map.110 = bf16[256,4096]{1,0:T(8,128)(2,1)S(1)} custom-call(s32[5]{0:T(128)S(1)} %stack.104.where_ref, bf16[2,128,1024]{2,1,0:T(8,128)(2,1)S(1)} %pad_maximum_fusion.1.q_ref, bf16[1024,128]{1,0:T(8,128)(2,1)S(1)} %get-tuple-element.50.k_ref, bf16[1024,256]{1,0:T(8,128)(2,1)S(1)} %concatenate.39.v_ref, bf16[512,4096]{1,0:T(8,128)(2,1)S(1)} %copy-done, ...), custom_call_target="tpu_custom_call" | custom-call | flops 2818572288 | bytes 8388608 | tf_op jit(solution)/shard_map/pallas_call | solution.py:77
  39.2 1.6 collective-permute-start.10
  41.1 1.2 collective-permute-start.12
  42.4 1.5 collective-permute-start.13
  43.9 2.2 %copy-done.1 = bf16[512,4096]{1,0:T(8,128)(2,1)S(1)} copy-done((bf16[512,4096]{1,0:T(8,128)(2,1)S(1)}, bf16[512,4096]{1,0:T(8,128)(2,1)}, u32[]{:S(2)}) %copy-start.1) | copy-done | bytes 4194328
  46.0 6.5 %shard_map.111 = f32[128,4096]{1,0:T(8,128)S(1)} custom-call(s32[5]{0:T(128)S(1)} %stack.87.where_ref, bf16[1,128,1024]{2,1,0:T(8,128)(2,1)S(1)} %maximum_bitcast_fusion.q_ref, bf16[1024,128]{1,0:T(8,128)(2,1)S(1)} %get-tuple-element.50.k_ref, bf16[1024,256]{1,0:T(8,128)(2,1)S(1)} %concatenate.39.v_ref, bf16[512,4096]{1,0:T(8,128)(2,1)S(1)} %copy-done.1, ...), custom_call_target="tpu_custom_call" | custom-call | flops 1409286144 | bytes 8388608 | tf_op jit(solution)/shard_map/pallas_call | solution.py:77
  52.6 1.2 convert_add_fusion.1
  53.9 8.3 %collective-permute-done.12 = bf16[128,2048]{1,0:T(8,128)(2,1)S(1)} collective-permute-done((bf16[128,2048]{1,0:T(8,128)(2,1)S(1)}, bf16[128,2048]{1,0:T(8,128)(2,1)S(1)}, u32[]{:S(2)}, u32[]{:S(2)}) %collective-permute-start.12) | collective-permute-done | bytes 524320 | tf_op jit(solution)/shard_map/ppermute | solution.py:195
  63.0 1.4 fusion
  64.3 59.3 %all_to_all.10 = bf16[64,8,4096]{2,1,0:T(8,128)(2,1)S(1)} all-to-all(bf16[64,8,4096]{2,1,0:T(8,128)(2,1)S(1)} %fusion), channel_id=1, replica_groups=mesh['group'=16,'y'=4,'core'=2] {'group','y'}, dimensions={0} | all-to-all | bytes 8388608 | tf_op jit(solution)/shard_map/all_to_all | solution.py:298
  123.6 4.5 %collective-permute-start.14 = (bf16[512,4096]{1,0:T(8,128)(2,1)S(1)}, bf16[512,4096]{1,0:T(8,128)(2,1)S(1)}, u32[]{:S(2)}, u32[]{:S(2)}) collective-permute-start(bf16[512,4096]{1,0:T(8,128)(2,1)S(1)} %bitcast.62), channel_id=1, source_target_pairs={{0,1},{1,0},{2,3},{3,2},{4,5},{5,4},{6,7},{7,6},{8,9},{9,8},{10,11... | collective-permute-start | bytes 12582920 | tf_op jit(solution)/shard_map/ppermute | solution.py:198
  128.2 7.2 %shard_map.112.a_ref = bf16[512,768]{1,0:T(8,128)(2,1)S(1)} custom-call(bf16[512,4096]{1,0:T(8,128)(2,1)S(1)} %bitcast.63, bf16[1,4096,768]{2,1,0:T(8,128)(2,1)S(1)} %bitcast.66, bf16[1,4096,768]{2,1,0:T(8,128)(2,1)S(1)} %bitcast.68), custom_call_target="tpu_custom_call" | custom-call | flops 6442450944 | bytes 16777216 | tf_op jit(solution)/shard_map/pallas_call | solution.py:118
  135.4 7.2 %shard_map.113.a_ref = bf16[512,768]{1,0:T(8,128)(2,1)S(1)} custom-call(bf16[512,4096]{1,0:T(8,128)(2,1)S(1)} %collective-permute-done.14.x_ref, bf16[1,4096,768]{2,1,0:T(8,128)(2,1)S(1)} %bitcast.66, bf16[1,4096,768]{2,1,0:T(8,128)(2,1)S(1)} %bitcast.68), custom_call_target="tpu_custom_call" | custom-call | flops 6442450944 | bytes 16777216 | tf_op jit(solution)/shard_map/pallas_call | solution.py:118
  151.9 56.8 %all_to_all.11 = bf16[64,8,4096]{2,1,0:T(8,128)(2,1)S(1)} all-to-all(bf16[64,8,4096]{2,1,0:T(8,128)(2,1)S(1)} %bitcast.61), channel_id=1, replica_groups=mesh['group'=16,'y'=4,'core'=2] {'group','y'}, dimensions={0} | all-to-all | bytes 8388608 | tf_op jit(solution)/shard_map/all_to_all | solution.py:310
  208.7 1.3 fusion.1
  210.0 1.4 fusion.3
  (104 shorter events, 20.1 us)
Async XLA Ops:
  0.0 17.0 %collective-permute-start.5 = (bf16[512,4096]{1,0:T(8,128)(2,1)}, bf16[512,4096]{1,0:T(8,128)(2,1)}, u32[]{:S(2)}, u32[]{:S(2)}) collective-permute-start(bf16[512,4096]{1,0:T(8,128)(2,1)} %own_ref.5), channel_id=1, source_target_pairs={{0,1},{1,0},{2,3},{3,2},{4,5},{5,4},{6,7},{7,6},{8,9},{9,8},{10,11... | collective-permute-start | bytes 12582920 | tf_op jit(solution)/shard_map/ppermute | solution.py:198
  2.4 8.6 %collective-permute-start.1 = (bf16[128,256]{1,0:T(8,128)(2,1)S(1)}, bf16[128,256]{1,0:T(8,128)(2,1)S(1)}, u32[]{:S(2)}, u32[]{:S(2)}) collective-permute-start(bf16[128,256]{1,0:T(8,128)(2,1)S(1)} %pad_maximum_fusion.7), channel_id=1, source_target_pairs={{0,6},{2,0},{4,2},{6,4},{1,7},{3,1},{5,3},{7,5},{8,14},{10,8},{12,... | collective-permute-start | bytes 196616 | tf_op jit(solution)/shard_map/ppermute | solution.py:195
  5.3 7.7 %collective-permute-start.2 = (bf16[128,256]{1,0:T(8,128)(2,1)S(1)}, bf16[128,256]{1,0:T(8,128)(2,1)S(1)}, u32[]{:S(2)}, u32[]{:S(2)}) collective-permute-start(bf16[128,256]{1,0:T(8,128)(2,1)S(1)} %pad_maximum_fusion.8), channel_id=1, source_target_pairs={{0,4},{2,6},{4,0},{6,2},{1,5},{3,7},{5,1},{7,3},{8,12},{10,14},{12... | collective-permute-start | bytes 196616 | tf_op jit(solution)/shard_map/ppermute | solution.py:195
  5.7 7.3 %collective-permute-start.3 = (bf16[128,256]{1,0:T(8,128)(2,1)S(1)}, bf16[128,256]{1,0:T(8,128)(2,1)S(1)}, u32[]{:S(2)}, u32[]{:S(2)}) collective-permute-start(bf16[128,256]{1,0:T(8,128)(2,1)S(1)} %pad_maximum_fusion.9), channel_id=1, source_target_pairs={{0,2},{2,4},{4,6},{6,0},{1,3},{3,5},{5,7},{7,1},{8,10},{10,12},{12... | collective-permute-start | bytes 196616 | tf_op jit(solution)/shard_map/ppermute | solution.py:195
  6.6 10.3 %collective-permute-start = (bf16[128,1024]{1,0:T(8,128)(2,1)S(1)}, bf16[128,1024]{1,0:T(8,128)(2,1)S(1)}, u32[]{:S(2)}, u32[]{:S(2)}) collective-permute-start(bf16[128,1024]{1,0:T(8,128)(2,1)S(1)} %pad_maximum_fusion.2), channel_id=1, source_target_pairs={{0,4},{2,6},{4,0},{6,2},{1,5},{3,7},{5,1},{7,3},{8,12},{10,14},{12... | collective-permute-start | bytes 786440 | tf_op jit(solution)/shard_map/ppermute | solution.py:195
  11.0 13.5 %collective-permute-start.8 = (bf16[128,1024]{1,0:T(8,128)(2,1)S(1)}, bf16[128,1024]{1,0:T(8,128)(2,1)S(1)}, u32[]{:S(2)}, u32[]{:S(2)}) collective-permute-start(bf16[128,1024]{1,0:T(8,128)(2,1)S(1)} %pad_maximum_fusion.4), channel_id=1, source_target_pairs={{0,6},{2,0},{4,2},{6,4},{1,7},{3,1},{5,3},{7,5},{8,14},{10,8},{12,... | collective-permute-start | bytes 786440 | tf_op jit(solution)/shard_map/ppermute | solution.py:195
  13.0 11.5 %collective-permute-start.9 = (bf16[128,1024]{1,0:T(8,128)(2,1)S(1)}, bf16[128,1024]{1,0:T(8,128)(2,1)S(1)}, u32[]{:S(2)}, u32[]{:S(2)}) collective-permute-start(bf16[128,1024]{1,0:T(8,128)(2,1)S(1)} %pad_maximum_fusion.5), channel_id=1, source_target_pairs={{0,2},{2,4},{4,6},{6,0},{1,3},{3,5},{5,7},{7,1},{8,10},{10,12},{12... | collective-permute-start | bytes 786440 | tf_op jit(solution)/shard_map/ppermute | solution.py:195
  13.1 2.9 %collective-permute-start.4 = (bf16[4,128,256]{2,1,0:T(8,128)(2,1)S(1)}, bf16[4,128,256]{2,1,0:T(8,128)(2,1)S(1)}, u32[]{:S(2)}, u32[]{:S(2)}) collective-permute-start(bf16[4,128,256]{2,1,0:T(8,128)(2,1)S(1)} %get-tuple-element.56), channel_id=1, source_target_pairs={{0,1},{1,0},{2,3},{3,2},{4,5},{5,4},{6,7},{7,6},{8,9},{9,8},{10,11... | collective-permute-start | bytes 786440 | tf_op jit(solution)/shard_map/ppermute | solution.py:198
  24.5 13.6 %collective-permute-start.6 = (bf16[128,2048]{1,0:T(8,128)(2,1)S(1)}, bf16[128,2048]{1,0:T(8,128)(2,1)S(1)}, u32[]{:S(2)}, u32[]{:S(2)}) collective-permute-start(bf16[128,2048]{1,0:T(8,128)(2,1)S(1)} %get-tuple-element.48), channel_id=1, source_target_pairs={{0,2},{2,4},{4,6},{6,0},{1,3},{3,5},{5,7},{7,1},{8,10},{10,12},{12... | collective-permute-start | bytes 1572872 | tf_op jit(solution)/shard_map/ppermute | solution.py:195
  25.2 12.9 %collective-permute-start.7 = (bf16[128,2048]{1,0:T(8,128)(2,1)S(1)}, bf16[128,2048]{1,0:T(8,128)(2,1)S(1)}, u32[]{:S(2)}, u32[]{:S(2)}) collective-permute-start(bf16[128,2048]{1,0:T(8,128)(2,1)S(1)} %get-tuple-element.47), channel_id=1, source_target_pairs={{0,6},{2,0},{4,2},{6,4},{1,7},{3,1},{5,3},{7,5},{8,14},{10,8},{12,... | collective-permute-start | bytes 1572872 | tf_op jit(solution)/shard_map/ppermute | solution.py:195
  36.9 15.7 %collective-permute-start.11 = (bf16[128,2048]{1,0:T(8,128)(2,1)S(1)}, bf16[128,2048]{1,0:T(8,128)(2,1)S(1)}, u32[]{:S(2)}, u32[]{:S(2)}) collective-permute-start(bf16[128,2048]{1,0:T(8,128)(2,1)S(1)} %get-tuple-element.37), channel_id=1, source_target_pairs={{0,6},{2,0},{4,2},{6,4},{1,7},{3,1},{5,3},{7,5},{8,14},{10,8},{12,... | collective-permute-start | bytes 1572872 | tf_op jit(solution)/shard_map/ppermute | solution.py:195
  39.2 13.4 %collective-permute-start.10 = (bf16[128,2048]{1,0:T(8,128)(2,1)}, bf16[128,2048]{1,0:T(8,128)(2,1)}, u32[]{:S(2)}, u32[]{:S(2)}) collective-permute-start(bf16[128,2048]{1,0:T(8,128)(2,1)} %get-tuple-element.35), channel_id=1, source_target_pairs={{0,2},{2,4},{4,6},{6,0},{1,3},{3,5},{5,7},{7,1},{8,10},{10,12},{12... | collective-permute-start | bytes 1572872 | tf_op jit(solution)/shard_map/ppermute | solution.py:195
  41.1 21.1 %collective-permute-start.12 = (bf16[128,2048]{1,0:T(8,128)(2,1)S(1)}, bf16[128,2048]{1,0:T(8,128)(2,1)S(1)}, u32[]{:S(2)}, u32[]{:S(2)}) collective-permute-start(bf16[128,2048]{1,0:T(8,128)(2,1)S(1)} %get-tuple-element.38), channel_id=1, source_target_pairs={{0,2},{2,4},{4,6},{6,0},{1,3},{3,5},{5,7},{7,1},{8,10},{10,12},{12... | collective-permute-start | bytes 1572872 | tf_op jit(solution)/shard_map/ppermute | solution.py:195
  42.4 19.8 %collective-permute-start.13 = (bf16[128,2048]{1,0:T(8,128)(2,1)S(1)}, bf16[128,2048]{1,0:T(8,128)(2,1)S(1)}, u32[]{:S(2)}, u32[]{:S(2)}) collective-permute-start(bf16[128,2048]{1,0:T(8,128)(2,1)S(1)} %get-tuple-element.36), channel_id=1, source_target_pairs={{0,6},{2,0},{4,2},{6,4},{1,7},{3,1},{5,3},{7,5},{8,14},{10,8},{12,... | collective-permute-start | bytes 1572872 | tf_op jit(solution)/shard_map/ppermute | solution.py:195
  62.3 65.8 %slice-start.2 = ((s8[6291456]{0:T(1024)(128)(4,1)}), s8[4194304]{0:T(1024)(128)(4,1)S(1)}, s32[]{:S(2)}) async-start(s8[6291456]{0:T(1024)(128)(4,1)} %bitcast.65), calls=%async_computation.4 | async-start | bytes 8388608
  62.4 65.8 %slice-start.4 = ((s8[6291456]{0:T(1024)(128)(4,1)}), s8[4194304]{0:T(1024)(128)(4,1)S(1)}, s32[]{:S(2)}) async-start(s8[6291456]{0:T(1024)(128)(4,1)} %bitcast.67), calls=%async_computation.6 | async-start | bytes 8388608
  62.9 65.2 %slice-start.3 = ((s8[6291456]{0:T(1024)(128)(4,1)}), s8[2097152]{0:T(1024)(128)(4,1)S(1)}, s32[]{:S(2)}) async-start(s8[6291456]{0:T(1024)(128)(4,1)} %bitcast.65), calls=%async_computation.5 | async-start | bytes 4194304
  62.9 65.2 %slice-start.5 = ((s8[6291456]{0:T(1024)(128)(4,1)}), s8[2097152]{0:T(1024)(128)(4,1)S(1)}, s32[]{:S(2)}) async-start(s8[6291456]{0:T(1024)(128)(4,1)} %bitcast.67), calls=%async_computation.7 | async-start | bytes 4194304
  64.3 78.2 %slice-start = ((s8[6291456]{0:T(1024)(128)(4,1)}), s8[4194304]{0:T(1024)(128)(4,1)S(1)}, s32[]{:S(2)}) async-start(s8[6291456]{0:T(1024)(128)(4,1)} %bitcast.59), calls=%async_computation.2 | async-start | bytes 8388608
  123.6 11.7 %collective-permute-start.14 = (bf16[512,4096]{1,0:T(8,128)(2,1)S(1)}, bf16[512,4096]{1,0:T(8,128)(2,1)S(1)}, u32[]{:S(2)}, u32[]{:S(2)}) collective-permute-start(bf16[512,4096]{1,0:T(8,128)(2,1)S(1)} %bitcast.62), channel_id=1, source_target_pairs={{0,1},{1,0},{2,3},{3,2},{4,5},{5,4},{6,7},{7,6},{8,9},{9,8},{10,11... | collective-permute-start | bytes 12582920 | tf_op jit(solution)/shard_map/ppermute | solution.py:198
  143.6 4.3 %collective-permute-start.18 = (bf16[512,1024]{1,0:T(8,128)(2,1)S(1)}, bf16[512,1024]{1,0:T(8,128)(2,1)S(1)}, u32[]{:S(2)}, u32[]{:S(2)}) collective-permute-start(bf16[512,1024]{1,0:T(8,128)(2,1)S(1)} %shard_map.117), channel_id=1, source_target_pairs={{0,1},{1,0},{2,3},{3,2},{4,5},{5,4},{6,7},{7,6},{8,9},{9,8},{10,11... | collective-permute-start | bytes 3145736 | tf_op jit(solution)/shard_map/ppermute | solution.py:198
  144.7 4.2 %collective-permute-start.17 = (bf16[512,1024]{1,0:T(8,128)(2,1)S(1)}, bf16[512,1024]{1,0:T(8,128)(2,1)S(1)}, u32[]{:S(2)}, u32[]{:S(2)}) collective-permute-start(bf16[512,1024]{1,0:T(8,128)(2,1)S(1)} %shard_map.116), channel_id=1, source_target_pairs={{0,1},{1,0},{2,3},{3,2},{4,5},{5,4},{6,7},{7,6},{8,9},{9,8},{10,11... | collective-permute-start | bytes 3145736 | tf_op jit(solution)/shard_map/ppermute | solution.py:198
  146.2 3.7 %collective-permute-start.16 = (bf16[512,1024]{1,0:T(8,128)(2,1)S(1)}, bf16[512,1024]{1,0:T(8,128)(2,1)S(1)}, u32[]{:S(2)}, u32[]{:S(2)}) collective-permute-start(bf16[512,1024]{1,0:T(8,128)(2,1)S(1)} %shard_map.115), channel_id=1, source_target_pairs={{0,1},{1,0},{2,3},{3,2},{4,5},{5,4},{6,7},{7,6},{8,9},{9,8},{10,11... | collective-permute-start | bytes 3145736 | tf_op jit(solution)/shard_map/ppermute | solution.py:198
  147.3 3.6 %collective-permute-start.15 = (bf16[512,1024]{1,0:T(8,128)(2,1)S(1)}, bf16[512,1024]{1,0:T(8,128)(2,1)S(1)}, u32[]{:S(2)}, u32[]{:S(2)}) collective-permute-start(bf16[512,1024]{1,0:T(8,128)(2,1)S(1)} %shard_map.114), channel_id=1, source_target_pairs={{0,1},{1,0},{2,3},{3,2},{4,5},{5,4},{6,7},{7,6},{8,9},{9,8},{10,11... | collective-permute-start | bytes 3145736 | tf_op jit(solution)/shard_map/ppermute | solution.py:198
  (8 other events, 57.5 us)

commit v2 on v1

--- a/solution.py
+++ b/solution.py
@@ -103,8 +103,8 @@
     return jnp.dot(a, b, preferred_element_type=jnp.float32)
 
 
-def gated_kernel(tile, x_ref, gate_ref, up_ref, o_ref):
-    @pl.loop(0, o_ref.shape[1] // tile)
+def gated_kernel(tile, unroll, x_ref, gate_ref, up_ref, o_ref):
+    @pl.loop(0, o_ref.shape[1] // tile, unroll=unroll)
     def _(step):
         at = pl.ds(pl.multiple_of(step * tile, tile), tile)
         gate = jnp.dot(x_ref[...], gate_ref[0, :, at], preferred_element_type=jnp.float32)
@@ -112,11 +112,11 @@
         o_ref[:, at] = (gate / (1.0 + jnp.exp(-gate)) * upward).astype(jnp.bfloat16)
 
 
-def gated(x, w_gate, w_up, tile=256):
+def gated(x, w_gate, w_up, unroll, tile=256):
     rows, depth = x.shape
     hidden = w_gate.shape[2]
     return pl.pallas_call(
-        functools.partial(gated_kernel, tile),
+        functools.partial(gated_kernel, tile, unroll),
         out_shape=jax.ShapeDtypeStruct((rows, hidden), jnp.bfloat16),
         in_specs=[pl.BlockSpec(memory_space=pltpu.VMEM)] * 3,
         out_specs=pl.BlockSpec(memory_space=pltpu.VMEM),
@@ -245,11 +245,11 @@
     keys = gathered[:, :HEAD]
     values = jnp.concatenate([gathered[:, HEAD:], jnp.ones_like(keys)], axis=1)
 
-    def attended(first, last, block, dtype, unroll):
+    def attended(first, last, block, dtype, unroll, tile=1024):
         places = [(y + step) % ring for step in ORDER[first:last]]
         places = places + [places[0]] * (ring - len(places)) + [core]
         places = jnp.stack(places).astype(jnp.int32)
-        return attend_project(places, block, keys, values, out_weight, weight_other, dtype, unroll)
+        return attend_project(places, block, keys, values, out_weight, weight_other, dtype, unroll, tile)
 
     opposite = attended(0, 1, jnp.stack(blocks[:1]), bf16, 4)
     from_left = along(opposite[:, :half], 1)
@@ -264,7 +264,7 @@
     right_sum = along((partial[:rows, :half].astype(f32) + from_left.astype(f32)).astype(bf16), 1)
     left_sum = along((partial[rows:, half:].astype(f32) + from_right.astype(f32)).astype(bf16), -1)
     last, _ = lax.optimization_barrier((jnp.stack(blocks[3:]), partial))
-    own = attended(3, 4, last, f32, 1)
+    own = attended(3, 4, last, f32, 1, 512)
     hidden = residual.astype(f32) + own
     hidden = hidden + jnp.concatenate(
         [
@@ -299,9 +299,9 @@
     mine = mine.reshape(experts * CAP, width)
     theirs = swap(mine)
 
-    active_mine = gated(mine, w_gate, w_up)
+    active_mine = gated(mine, w_gate, w_up, 1)
     theirs, active_mine = lax.optimization_barrier((theirs, active_mine))
-    active_theirs = gated(theirs, w_gate, w_up)
+    active_theirs = gated(theirs, w_gate, w_up, 3)
     back = [swap(down(active_theirs, w_down, side)) for side in range(PARTS)]
     expert_out = None
     for side in range(PARTS):

time: 213 us -> 213 us (level)
  transfers between devices with their start and end apart: 19 -> 19, of which waited for: 4 -> 4; matrix products, arithmetic and copies ran while one was open for 3% -> 3% of each run, Pallas kernels for 17% -> 18%
where the time goes in v2:
time: 213 us; the launch traced here: 211 us
  blocking collectives  116 us (54%)
  Pallas kernels  45.7 us (21%)
  starting transfers between devices  25 us (12%)
  waiting for transfers between devices  8.66 us (4%)
  local copies, waits for them, and re-layouts  6.2 us (3%)
  other arithmetic  6.13 us (3%)
  matrix products  2.61 us (1%)
    all_to_all x1, blocking collectives, local(): lax.all_to_all(slots, ('group', 'y'), split_axis=0, concat_axis=0, tiled=...  59.3 us
    all_to_all x1, blocking collectives, local(): lax.all_to_all(expert_out.reshape(experts, CAP, width), ('group', 'y'), s...  56.8 us
    pallas_call x3, Pallas kernels, attend_project(): pl.pallas_call(functools.partial(attend_project_kernel, unroll), out_shap...  23.9 us
    ppermute x12, starting transfers between devices, along(): lax.ppermute(value, 'y', [(i, (i + step) % ring) for i in range(ring)])  15.9 us
    pallas_call x2, Pallas kernels, gated(): pl.pallas_call(functools.partial(gated_kernel, tile, unroll), out_shape=j...  13.9 us
    ppermute x7, starting transfers between devices, swap(): return lax.ppermute(value, 'core', [(0, 1), (1, 0)])  9.03 us
    pallas_call x8, Pallas kernels, down(): pl.pallas_call(functools.partial(down_kernel, tile, side, side * width //...  7.9 us
    ppermute x12, waiting for transfers between devices, along(): lax.ppermute(value, 'y', [(i, (i + step) % ring) for i in range(ring)])  7.66 us
  transfers between devices with their start and end apart: 19, of which 4 were waited for; matrix products, arithmetic and copies ran while one was open for 3% of the time, Pallas kernels for 18%

profile of v2, /device:TPU:1, one launch (start us, length us, event | category | flops | bytes accessed | tf_op | source)
XLA Modules:
  0.0 210.8 jit_solution(6571092477686336287)
XLA Ops:
  0.0 1.4 collective-permute-start.5
  2.4 2.9 %collective-permute-start.1 = (bf16[128,256]{1,0:T(8,128)(2,1)S(1)}, bf16[128,256]{1,0:T(8,128)(2,1)S(1)}, u32[]{:S(2)}, u32[]{:S(2)}) collective-permute-start(bf16[128,256]{1,0:T(8,128)(2,1)S(1)} %pad_maximum_fusion.7), channel_id=1, source_target_pairs={{0,6},{2,0},{4,2},{6,4},{1,7},{3,1},{5,3},{7,5},{8,14},{10,8},{12,... | collective-permute-start | bytes 196616 | tf_op jit(solution)/shard_map/ppermute | solution.py:195
  6.6 2.1 %collective-permute-start = (bf16[128,1024]{1,0:T(8,128)(2,1)S(1)}, bf16[128,1024]{1,0:T(8,128)(2,1)S(1)}, u32[]{:S(2)}, u32[]{:S(2)}) collective-permute-start(bf16[128,1024]{1,0:T(8,128)(2,1)S(1)} %pad_maximum_fusion.2), channel_id=1, source_target_pairs={{0,4},{2,6},{4,0},{6,2},{1,5},{3,7},{5,1},{7,3},{8,12},{10,14},{12... | collective-permute-start | bytes 786440 | tf_op jit(solution)/shard_map/ppermute | solution.py:195
  11.0 2.0 collective-permute-start.8
  13.1 1.8 collective-permute-start.4
  17.0 1.3 copy-done
  18.3 6.1 %shard_map.109 = bf16[128,4096]{1,0:T(8,128)(2,1)S(1)} custom-call(s32[5]{0:T(128)S(1)} %stack.90.where_ref, bf16[1,128,1024]{2,1,0:T(8,128)(2,1)S(1)} %bitcast.64, bf16[1024,128]{1,0:T(8,128)(2,1)S(1)} %get-tuple-element.50.k_ref, bf16[1024,256]{1,0:T(8,128)(2,1)S(1)} %concatenate.39.v_ref, bf16[512,4096]{1,0:T(8,128)(2,1)S(1)} %copy-done, ...), custom_call_target="tpu_custom_call" | custom-call | flops 1409286144 | bytes 8388608 | tf_op jit(solution)/shard_map/pallas_call | solution.py:77
  25.2 2.2 %collective-permute-start.7 = (bf16[128,2048]{1,0:T(8,128)(2,1)S(1)}, bf16[128,2048]{1,0:T(8,128)(2,1)S(1)}, u32[]{:S(2)}, u32[]{:S(2)}) collective-permute-start(bf16[128,2048]{1,0:T(8,128)(2,1)S(1)} %get-tuple-element.47), channel_id=1, source_target_pairs={{0,6},{2,0},{4,2},{6,4},{1,7},{3,1},{5,3},{7,5},{8,14},{10,8},{12,... | collective-permute-start | bytes 1572872 | tf_op jit(solution)/shard_map/ppermute | solution.py:195
  27.4 9.3 %shard_map.110 = bf16[256,4096]{1,0:T(8,128)(2,1)S(1)} custom-call(s32[5]{0:T(128)S(1)} %stack.104.where_ref, bf16[2,128,1024]{2,1,0:T(8,128)(2,1)S(1)} %pad_maximum_fusion.1.q_ref, bf16[1024,128]{1,0:T(8,128)(2,1)S(1)} %get-tuple-element.50.k_ref, bf16[1024,256]{1,0:T(8,128)(2,1)S(1)} %concatenate.39.v_ref, bf16[512,4096]{1,0:T(8,128)(2,1)S(1)} %copy-done, ...), custom_call_target="tpu_custom_call" | custom-call | flops 2818572288 | bytes 8388608 | tf_op jit(solution)/shard_map/pallas_call | solution.py:77
  39.2 1.6 collective-permute-start.10
  41.1 1.2 collective-permute-start.12
  42.4 1.5 collective-permute-start.13
  43.9 2.2 %copy-done.1 = bf16[512,4096]{1,0:T(8,128)(2,1)S(1)} copy-done((bf16[512,4096]{1,0:T(8,128)(2,1)S(1)}, bf16[512,4096]{1,0:T(8,128)(2,1)}, u32[]{:S(2)}) %copy-start.1) | copy-done | bytes 4194328
  46.0 8.5 %shard_map.111 = f32[128,4096]{1,0:T(8,128)S(1)} custom-call(s32[5]{0:T(128)S(1)} %stack.87.where_ref, bf16[1,128,1024]{2,1,0:T(8,128)(2,1)S(1)} %maximum_bitcast_fusion.q_ref, bf16[1024,128]{1,0:T(8,128)(2,1)S(1)} %get-tuple-element.50.k_ref, bf16[1024,256]{1,0:T(8,128)(2,1)S(1)} %concatenate.39.v_ref, bf16[512,4096]{1,0:T(8,128)(2,1)S(1)} %copy-done.1, ...), custom_call_target="tpu_custom_call" | custom-call | flops 1409286144 | bytes 8388608 | tf_op jit(solution)/shard_map/pallas_call | solution.py:77
  54.6 1.2 convert_add_fusion.1
  55.8 6.4 %collective-permute-done.12 = bf16[128,2048]{1,0:T(8,128)(2,1)S(1)} collective-permute-done((bf16[128,2048]{1,0:T(8,128)(2,1)S(1)}, bf16[128,2048]{1,0:T(8,128)(2,1)S(1)}, u32[]{:S(2)}, u32[]{:S(2)}) %collective-permute-start.12) | collective-permute-done | bytes 524320 | tf_op jit(solution)/shard_map/ppermute | solution.py:195
  63.0 1.4 fusion
  64.3 59.3 %all_to_all.10 = bf16[64,8,4096]{2,1,0:T(8,128)(2,1)S(1)} all-to-all(bf16[64,8,4096]{2,1,0:T(8,128)(2,1)S(1)} %fusion), channel_id=1, replica_groups=mesh['group'=16,'y'=4,'core'=2] {'group','y'}, dimensions={0} | all-to-all | bytes 8388608 | tf_op jit(solution)/shard_map/all_to_all | solution.py:298
  123.6 4.5 %collective-permute-start.14 = (bf16[512,4096]{1,0:T(8,128)(2,1)S(1)}, bf16[512,4096]{1,0:T(8,128)(2,1)S(1)}, u32[]{:S(2)}, u32[]{:S(2)}) collective-permute-start(bf16[512,4096]{1,0:T(8,128)(2,1)S(1)} %bitcast.62), channel_id=1, source_target_pairs={{0,1},{1,0},{2,3},{3,2},{4,5},{5,4},{6,7},{7,6},{8,9},{9,8},{10,11... | collective-permute-start | bytes 12582920 | tf_op jit(solution)/shard_map/ppermute | solution.py:198
  128.2 7.2 %shard_map.112.a_ref = bf16[512,768]{1,0:T(8,128)(2,1)S(1)} custom-call(bf16[512,4096]{1,0:T(8,128)(2,1)S(1)} %bitcast.63, bf16[1,4096,768]{2,1,0:T(8,128)(2,1)S(1)} %bitcast.66, bf16[1,4096,768]{2,1,0:T(8,128)(2,1)S(1)} %bitcast.68), custom_call_target="tpu_custom_call" | custom-call | flops 6442450944 | bytes 16777216 | tf_op jit(solution)/shard_map/pallas_call | solution.py:118
  135.4 6.7 %shard_map.113.a_ref = bf16[512,768]{1,0:T(8,128)(2,1)S(1)} custom-call(bf16[512,4096]{1,0:T(8,128)(2,1)S(1)} %collective-permute-done.14.x_ref, bf16[1,4096,768]{2,1,0:T(8,128)(2,1)S(1)} %bitcast.66, bf16[1,4096,768]{2,1,0:T(8,128)(2,1)S(1)} %bitcast.68), custom_call_target="tpu_custom_call" | custom-call | flops 6442450944 | bytes 16777216 | tf_op jit(solution)/shard_map/pallas_call | solution.py:118
  151.4 56.8 %all_to_all.11 = bf16[64,8,4096]{2,1,0:T(8,128)(2,1)S(1)} all-to-all(bf16[64,8,4096]{2,1,0:T(8,128)(2,1)S(1)} %bitcast.61), channel_id=1, replica_groups=mesh['group'=16,'y'=4,'core'=2] {'group','y'}, dimensions={0} | all-to-all | bytes 8388608 | tf_op jit(solution)/shard_map/all_to_all | solution.py:310
  208.2 1.3 fusion.1
  209.4 1.4 fusion.3
  (104 shorter events, 20.1 us)
Async XLA Ops:
  0.0 17.0 %collective-permute-start.5 = (bf16[512,4096]{1,0:T(8,128)(2,1)}, bf16[512,4096]{1,0:T(8,128)(2,1)}, u32[]{:S(2)}, u32[]{:S(2)}) collective-permute-start(bf16[512,4096]{1,0:T(8,128)(2,1)} %own_ref.5), channel_id=1, source_target_pairs={{0,1},{1,0},{2,3},{3,2},{4,5},{5,4},{6,7},{7,6},{8,9},{9,8},{10,11... | collective-permute-start | bytes 12582920 | tf_op jit(solution)/shard_map/ppermute | solution.py:198
  2.4 8.6 %collective-permute-start.1 = (bf16[128,256]{1,0:T(8,128)(2,1)S(1)}, bf16[128,256]{1,0:T(8,128)(2,1)S(1)}, u32[]{:S(2)}, u32[]{:S(2)}) collective-permute-start(bf16[128,256]{1,0:T(8,128)(2,1)S(1)} %pad_maximum_fusion.7), channel_id=1, source_target_pairs={{0,6},{2,0},{4,2},{6,4},{1,7},{3,1},{5,3},{7,5},{8,14},{10,8},{12,... | collective-permute-start | bytes 196616 | tf_op jit(solution)/shard_map/ppermute | solution.py:195
  5.3 7.7 %collective-permute-start.2 = (bf16[128,256]{1,0:T(8,128)(2,1)S(1)}, bf16[128,256]{1,0:T(8,128)(2,1)S(1)}, u32[]{:S(2)}, u32[]{:S(2)}) collective-permute-start(bf16[128,256]{1,0:T(8,128)(2,1)S(1)} %pad_maximum_fusion.8), channel_id=1, source_target_pairs={{0,4},{2,6},{4,0},{6,2},{1,5},{3,7},{5,1},{7,3},{8,12},{10,14},{12... | collective-permute-start | bytes 196616 | tf_op jit(solution)/shard_map/ppermute | solution.py:195
  5.7 7.3 %collective-permute-start.3 = (bf16[128,256]{1,0:T(8,128)(2,1)S(1)}, bf16[128,256]{1,0:T(8,128)(2,1)S(1)}, u32[]{:S(2)}, u32[]{:S(2)}) collective-permute-start(bf16[128,256]{1,0:T(8,128)(2,1)S(1)} %pad_maximum_fusion.9), channel_id=1, source_target_pairs={{0,2},{2,4},{4,6},{6,0},{1,3},{3,5},{5,7},{7,1},{8,10},{10,12},{12... | collective-permute-start | bytes 196616 | tf_op jit(solution)/shard_map/ppermute | solution.py:195
  6.6 10.3 %collective-permute-start = (bf16[128,1024]{1,0:T(8,128)(2,1)S(1)}, bf16[128,1024]{1,0:T(8,128)(2,1)S(1)}, u32[]{:S(2)}, u32[]{:S(2)}) collective-permute-start(bf16[128,1024]{1,0:T(8,128)(2,1)S(1)} %pad_maximum_fusion.2), channel_id=1, source_target_pairs={{0,4},{2,6},{4,0},{6,2},{1,5},{3,7},{5,1},{7,3},{8,12},{10,14},{12... | collective-permute-start | bytes 786440 | tf_op jit(solution)/shard_map/ppermute | solution.py:195
  11.0 13.5 %collective-permute-start.8 = (bf16[128,1024]{1,0:T(8,128)(2,1)S(1)}, bf16[128,1024]{1,0:T(8,128)(2,1)S(1)}, u32[]{:S(2)}, u32[]{:S(2)}) collective-permute-start(bf16[128,1024]{1,0:T(8,128)(2,1)S(1)} %pad_maximum_fusion.4), channel_id=1, source_target_pairs={{0,6},{2,0},{4,2},{6,4},{1,7},{3,1},{5,3},{7,5},{8,14},{10,8},{12,... | collective-permute-start | bytes 786440 | tf_op jit(solution)/shard_map/ppermute | solution.py:195
  13.0 11.5 %collective-permute-start.9 = (bf16[128,1024]{1,0:T(8,128)(2,1)S(1)}, bf16[128,1024]{1,0:T(8,128)(2,1)S(1)}, u32[]{:S(2)}, u32[]{:S(2)}) collective-permute-start(bf16[128,1024]{1,0:T(8,128)(2,1)S(1)} %pad_maximum_fusion.5), channel_id=1, source_target_pairs={{0,2},{2,4},{4,6},{6,0},{1,3},{3,5},{5,7},{7,1},{8,10},{10,12},{12... | collective-permute-start | bytes 786440 | tf_op jit(solution)/shard_map/ppermute | solution.py:195
  13.1 2.9 %collective-permute-start.4 = (bf16[4,128,256]{2,1,0:T(8,128)(2,1)S(1)}, bf16[4,128,256]{2,1,0:T(8,128)(2,1)S(1)}, u32[]{:S(2)}, u32[]{:S(2)}) collective-permute-start(bf16[4,128,256]{2,1,0:T(8,128)(2,1)S(1)} %get-tuple-element.56), channel_id=1, source_target_pairs={{0,1},{1,0},{2,3},{3,2},{4,5},{5,4},{6,7},{7,6},{8,9},{9,8},{10,11... | collective-permute-start | bytes 786440 | tf_op jit(solution)/shard_map/ppermute | solution.py:198
  24.5 13.6 %collective-permute-start.6 = (bf16[128,2048]{1,0:T(8,128)(2,1)S(1)}, bf16[128,2048]{1,0:T(8,128)(2,1)S(1)}, u32[]{:S(2)}, u32[]{:S(2)}) collective-permute-start(bf16[128,2048]{1,0:T(8,128)(2,1)S(1)} %get-tuple-element.48), channel_id=1, source_target_pairs={{0,2},{2,4},{4,6},{6,0},{1,3},{3,5},{5,7},{7,1},{8,10},{10,12},{12... | collective-permute-start | bytes 1572872 | tf_op jit(solution)/shard_map/ppermute | solution.py:195
  25.2 12.9 %collective-permute-start.7 = (bf16[128,2048]{1,0:T(8,128)(2,1)S(1)}, bf16[128,2048]{1,0:T(8,128)(2,1)S(1)}, u32[]{:S(2)}, u32[]{:S(2)}) collective-permute-start(bf16[128,2048]{1,0:T(8,128)(2,1)S(1)} %get-tuple-element.47), channel_id=1, source_target_pairs={{0,6},{2,0},{4,2},{6,4},{1,7},{3,1},{5,3},{7,5},{8,14},{10,8},{12,... | collective-permute-start | bytes 1572872 | tf_op jit(solution)/shard_map/ppermute | solution.py:195
  36.9 17.7 %collective-permute-start.11 = (bf16[128,2048]{1,0:T(8,128)(2,1)S(1)}, bf16[128,2048]{1,0:T(8,128)(2,1)S(1)}, u32[]{:S(2)}, u32[]{:S(2)}) collective-permute-start(bf16[128,2048]{1,0:T(8,128)(2,1)S(1)} %get-tuple-element.37), channel_id=1, source_target_pairs={{0,6},{2,0},{4,2},{6,4},{1,7},{3,1},{5,3},{7,5},{8,14},{10,8},{12,... | collective-permute-start | bytes 1572872 | tf_op jit(solution)/shard_map/ppermute | solution.py:195
  39.2 15.4 %collective-permute-start.10 = (bf16[128,2048]{1,0:T(8,128)(2,1)}, bf16[128,2048]{1,0:T(8,128)(2,1)}, u32[]{:S(2)}, u32[]{:S(2)}) collective-permute-start(bf16[128,2048]{1,0:T(8,128)(2,1)} %get-tuple-element.35), channel_id=1, source_target_pairs={{0,2},{2,4},{4,6},{6,0},{1,3},{3,5},{5,7},{7,1},{8,10},{10,12},{12... | collective-permute-start | bytes 1572872 | tf_op jit(solution)/shard_map/ppermute | solution.py:195
  41.1 21.1 %collective-permute-start.12 = (bf16[128,2048]{1,0:T(8,128)(2,1)S(1)}, bf16[128,2048]{1,0:T(8,128)(2,1)S(1)}, u32[]{:S(2)}, u32[]{:S(2)}) collective-permute-start(bf16[128,2048]{1,0:T(8,128)(2,1)S(1)} %get-tuple-element.38), channel_id=1, source_target_pairs={{0,2},{2,4},{4,6},{6,0},{1,3},{3,5},{5,7},{7,1},{8,10},{10,12},{12... | collective-permute-start | bytes 1572872 | tf_op jit(solution)/shard_map/ppermute | solution.py:195
  42.4 19.8 %collective-permute-start.13 = (bf16[128,2048]{1,0:T(8,128)(2,1)S(1)}, bf16[128,2048]{1,0:T(8,128)(2,1)S(1)}, u32[]{:S(2)}, u32[]{:S(2)}) collective-permute-start(bf16[128,2048]{1,0:T(8,128)(2,1)S(1)} %get-tuple-element.36), channel_id=1, source_target_pairs={{0,6},{2,0},{4,2},{6,4},{1,7},{3,1},{5,3},{7,5},{8,14},{10,8},{12,... | collective-permute-start | bytes 1572872 | tf_op jit(solution)/shard_map/ppermute | solution.py:195
  62.3 65.8 %slice-start.2 = ((s8[6291456]{0:T(1024)(128)(4,1)}), s8[4194304]{0:T(1024)(128)(4,1)S(1)}, s32[]{:S(2)}) async-start(s8[6291456]{0:T(1024)(128)(4,1)} %bitcast.65), calls=%async_computation.4 | async-start | bytes 8388608
  62.4 65.8 %slice-start.4 = ((s8[6291456]{0:T(1024)(128)(4,1)}), s8[4194304]{0:T(1024)(128)(4,1)S(1)}, s32[]{:S(2)}) async-start(s8[6291456]{0:T(1024)(128)(4,1)} %bitcast.67), calls=%async_computation.6 | async-start | bytes 8388608
  62.9 65.2 %slice-start.3 = ((s8[6291456]{0:T(1024)(128)(4,1)}), s8[2097152]{0:T(1024)(128)(4,1)S(1)}, s32[]{:S(2)}) async-start(s8[6291456]{0:T(1024)(128)(4,1)} %bitcast.65), calls=%async_computation.5 | async-start | bytes 4194304
  62.9 65.2 %slice-start.5 = ((s8[6291456]{0:T(1024)(128)(4,1)}), s8[2097152]{0:T(1024)(128)(4,1)S(1)}, s32[]{:S(2)}) async-start(s8[6291456]{0:T(1024)(128)(4,1)} %bitcast.67), calls=%async_computation.7 | async-start | bytes 4194304
  64.3 77.7 %slice-start = ((s8[6291456]{0:T(1024)(128)(4,1)}), s8[4194304]{0:T(1024)(128)(4,1)S(1)}, s32[]{:S(2)}) async-start(s8[6291456]{0:T(1024)(128)(4,1)} %bitcast.59), calls=%async_computation.2 | async-start | bytes 8388608
  123.6 11.7 %collective-permute-start.14 = (bf16[512,4096]{1,0:T(8,128)(2,1)S(1)}, bf16[512,4096]{1,0:T(8,128)(2,1)S(1)}, u32[]{:S(2)}, u32[]{:S(2)}) collective-permute-start(bf16[512,4096]{1,0:T(8,128)(2,1)S(1)} %bitcast.62), channel_id=1, source_target_pairs={{0,1},{1,0},{2,3},{3,2},{4,5},{5,4},{6,7},{7,6},{8,9},{9,8},{10,11... | collective-permute-start | bytes 12582920 | tf_op jit(solution)/shard_map/ppermute | solution.py:198
  143.0 4.3 %collective-permute-start.18 = (bf16[512,1024]{1,0:T(8,128)(2,1)S(1)}, bf16[512,1024]{1,0:T(8,128)(2,1)S(1)}, u32[]{:S(2)}, u32[]{:S(2)}) collective-permute-start(bf16[512,1024]{1,0:T(8,128)(2,1)S(1)} %shard_map.117), channel_id=1, source_target_pairs={{0,1},{1,0},{2,3},{3,2},{4,5},{5,4},{6,7},{7,6},{8,9},{9,8},{10,11... | collective-permute-start | bytes 3145736 | tf_op jit(solution)/shard_map/ppermute | solution.py:198
  144.1 4.2 %collective-permute-start.17 = (bf16[512,1024]{1,0:T(8,128)(2,1)S(1)}, bf16[512,1024]{1,0:T(8,128)(2,1)S(1)}, u32[]{:S(2)}, u32[]{:S(2)}) collective-permute-start(bf16[512,1024]{1,0:T(8,128)(2,1)S(1)} %shard_map.116), channel_id=1, source_target_pairs={{0,1},{1,0},{2,3},{3,2},{4,5},{5,4},{6,7},{7,6},{8,9},{9,8},{10,11... | collective-permute-start | bytes 3145736 | tf_op jit(solution)/shard_map/ppermute | solution.py:198
  145.7 3.7 %collective-permute-start.16 = (bf16[512,1024]{1,0:T(8,128)(2,1)S(1)}, bf16[512,1024]{1,0:T(8,128)(2,1)S(1)}, u32[]{:S(2)}, u32[]{:S(2)}) collective-permute-start(bf16[512,1024]{1,0:T(8,128)(2,1)S(1)} %shard_map.115), channel_id=1, source_target_pairs={{0,1},{1,0},{2,3},{3,2},{4,5},{5,4},{6,7},{7,6},{8,9},{9,8},{10,11... | collective-permute-start | bytes 3145736 | tf_op jit(solution)/shard_map/ppermute | solution.py:198
  146.8 3.6 %collective-permute-start.15 = (bf16[512,1024]{1,0:T(8,128)(2,1)S(1)}, bf16[512,1024]{1,0:T(8,128)(2,1)S(1)}, u32[]{:S(2)}, u32[]{:S(2)}) collective-permute-start(bf16[512,1024]{1,0:T(8,128)(2,1)S(1)} %shard_map.114), channel_id=1, source_target_pairs={{0,1},{1,0},{2,3},{3,2},{4,5},{5,4},{6,7},{7,6},{8,9},{9,8},{10,11... | collective-permute-start | bytes 3145736 | tf_op jit(solution)/shard_map/ppermute | solution.py:198
  (8 other events, 55.0 us)
